TPU v7x, 32 devices: a whole 2x2x4 slice. The times are simulated.
32 devices in a mesh: groups: 2 (over x), blk: 16 (over z, y, core).
Axes of the slice: x: 2, y: 2, z: 4, core: 2. Of those that a mesh axis runs over, the one named last changes fastest.
Arguments:
- embeddings: bfloat16 [16384, 768], P(('groups', 'blk')), parts along dimension 0
- doc_order: int32 [16384], P(('groups', 'blk')), parts along dimension 0, may hold values from 0 to 8191, each once
- neighbours: int32 [32, 4], P('groups'), parts along dimension 0, may hold values from 0 to 15, as said below
Outputs:
- earlier_max: float32 [16384], P(('groups', 'blk')), parts along dimension 0
- later_max: bfloat16 [16384], P(('groups', 'blk')), parts along dimension 0
There are 2 independent parts, one for each index of `groups`. A program takes and returns all parts, laid end to end along the dimension named above; each array names one. Nothing has to cross between parts.
Inputs may be any that keep to these rules, and one draw needn't show every extreme that they name: Every entry of neighbours[b] is a block at distance at most 2 from b along the loop of 16 blocks, (b + k) mod 16 with -2 <= k <= 2; block 0 lists both blocks at distance 2; a block may list an entry several times or list itself.
All inputs are finite; a program needn't handle non-finite values.
Results may differ from a plain program's by a relative error of at most 0.0028.
Values may be sent and summed in bfloat16 or wider, within the bound.
A program may use at most 64 MiB of HBM per device.

v0:
```python
import jax
import jax.numpy as jnp
from jax import lax
from jax.sharding import PartitionSpec as P

REACH = 2


def from_behind(x, axis, by):
    peers = lax.axis_size(axis)
    return lax.ppermute(x, axis, [(i, (i + by) % peers) for i in range(peers)])


def normalize(embeddings):
    values = embeddings.astype(jnp.float32)
    inverse = lax.rsqrt(jnp.sum(values * values, axis=-1, keepdims=True) + 1e-06)
    return (values * inverse).astype(jnp.bfloat16)


def pair_scores(unit_rows, order_rows, unit_cols, order_cols, listed):
    scores = lax.dot_general(
        unit_rows, unit_cols, (((1,), (1,)), ((), ())), preferred_element_type=jnp.float32
    )
    valid = jnp.logical_and(order_cols[None, :] < order_rows[:, None], listed)
    return jnp.where(valid, scores, jnp.float32(-1.0))


def local(embeddings, doc_order, neighbours):
    rows_now = embeddings.shape[0]
    blocks = lax.axis_size("blk")
    here = lax.axis_index("blk")
    unit_rows = normalize(embeddings)
    my_list = lax.dynamic_index_in_dim(neighbours, here, 0, keepdims=False)

    def visit(row_best, unit_cols, order_cols, block_id):
        listed = jnp.any(my_list == block_id)
        masked = pair_scores(unit_rows, doc_order, unit_cols, order_cols, listed)
        return (
            jnp.maximum(row_best, jnp.max(masked, axis=1)),
            jnp.max(masked, axis=0).astype(jnp.bfloat16),
        )

    own_masked = pair_scores(unit_rows, doc_order, unit_rows, doc_order, True)
    row_best = jnp.max(own_masked, axis=1)
    later = jnp.max(own_masked, axis=0).astype(jnp.bfloat16)
    empty_col = jnp.full((rows_now,), -1.0, jnp.bfloat16)
    up_units, up_order, up_travel = (unit_rows, doc_order, empty_col)
    for step in range(1, REACH + 1):
        up_units, up_order, up_travel = from_behind((up_units, up_order, up_travel), "blk", 1)
        row_best, col_part = visit(row_best, up_units, up_order, (here - step) % blocks)
        up_travel = jnp.maximum(up_travel, col_part)
    down_units, down_order, down_travel = (unit_rows, doc_order, empty_col)
    for step in range(1, REACH + 1):
        down_units, down_order, down_travel = from_behind(
            (down_units, down_order, down_travel), "blk", -1
        )
        row_best, col_part = visit(row_best, down_units, down_order, (here + step) % blocks)
        down_travel = jnp.maximum(down_travel, col_part)
    later = jnp.maximum(later, from_behind(up_travel, "blk", -REACH))
    later = jnp.maximum(later, from_behind(down_travel, "blk", REACH))
    return (row_best, later)


def solution(mesh):
    placed = (P(("groups", "blk"), None), P(("groups", "blk")), P("groups", None))
    return jax.shard_map(
        local,
        mesh=mesh,
        in_specs=placed,
        out_specs=(P(("groups", "blk")), P(("groups", "blk"))),
        check_vma=False,
    )
```

profile of v0, /device:TPU:0, one launch (start us, length us, event | category | flops | bytes accessed | tf_op | source)
XLA Modules:
  0.0 63.2 jit_solution(10614746640065709251)
XLA Ops:
  0.7 1.4 %fusion = f32[512]{0:T(512)S(1)} fusion(bf16[512,768]{1,0:T(8,128)(2,1)} %param.3), kind=kLoop, calls=%fused_computation.2 | loop fusion | flops 1179136 | bytes 788480 | tf_op jit(solution)/shard_map/reduce_sum | solution.py:16
  2.3 5.5 %collective-permute-start.5 = (bf16[512,768]{1,0:T(8,128)(2,1)S(1)}, bf16[512,768]{1,0:T(8,128)(2,1)S(1)}, u32[]{:S(2)}, u32[]{:S(2)}) collective-permute-start(bf16[512,768]{1,0:T(8,128)(2,1)S(1)} %fusion.1), channel_id=1, source_target_pairs={{0,15},{1,0},{2,1},{3,2},{4,3},{5,4},{6,5},{7,6},{8,7},{9,8},{10,9... | collective-permute-start | bytes 2359304 | tf_op jit(solution)/shard_map/ppermute | solution.py:11
  7.8 9.5 %collective-permute-done.5 = bf16[512,768]{1,0:T(8,128)(2,1)S(1)} collective-permute-done((bf16[512,768]{1,0:T(8,128)(2,1)S(1)}, bf16[512,768]{1,0:T(8,128)(2,1)S(1)}, u32[]{:S(2)}, u32[]{:S(2)}) %collective-permute-start.5) | collective-permute-done | bytes 786464 | tf_op jit(solution)/shard_map/ppermute | solution.py:11
  17.3 4.7 %collective-permute-start.7 = (bf16[512,768]{1,0:T(8,128)(2,1)S(1)}, bf16[512,768]{1,0:T(8,128)(2,1)S(1)}, u32[]{:S(2)}, u32[]{:S(2)}) collective-permute-start(bf16[512,768]{1,0:T(8,128)(2,1)S(1)} %collective-permute-done.5), channel_id=1, source_target_pairs={{0,15},{1,0},{2,1},{3,2},{4,3},{5,4},{6,5},{7,6},{8,7},{9,8},{10,9... | collective-permute-start | bytes 2359304 | tf_op jit(solution)/shard_map/ppermute | solution.py:11
  22.0 1.5 %collective-permute-start = (s32[512]{0:T(512)S(1)}, s32[512]{0:T(512)S(1)}, u32[]{:S(2)}, u32[]{:S(2)}) collective-permute-start(s32[512]{0:T(512)S(1)} %copy-done.2), channel_id=1, source_target_pairs={{0,1},{1,2},{2,3},{3,4},{4,5},{5,6},{6,7},{7,8},{8,9},{9,10},{10,1... | collective-permute-start | bytes 6152 | tf_op jit(solution)/shard_map/ppermute | solution.py:11
  23.6 2.9 %collective-permute-start.4 = (s32[512]{0:T(512)S(1)}, s32[512]{0:T(512)S(1)}, u32[]{:S(2)}, u32[]{:S(2)}) collective-permute-start(s32[512]{0:T(512)S(1)} %copy-done.2), channel_id=1, source_target_pairs={{0,15},{1,0},{2,1},{3,2},{4,3},{5,4},{6,5},{7,6},{8,7},{9,8},{10,9... | collective-permute-start | bytes 6152 | tf_op jit(solution)/shard_map/ppermute | solution.py:11
  26.5 0.8 %compare_reduce_fusion.3 = (pred[]{:T(512)}, pred[]{:T(512)}, pred[]{:T(512)}, pred[]{:T(512)}) fusion(s32[]{:T(128)S(6)} %select_n.41, s32[16,4]{0,1:T(4,128)S(1)} %copy-done.1, s32[]{:T(128)S(6)} %select_n.40, s32[]{:T(128)S(6)} %select_n.43, s32[]{:T(128)S(6)} %select_n.45, s32[]{:T(128)S(6)} %select_n.47), kind=kLoop, calls=%fused_computation.22 | loop fusion | flops 28 | bytes 40 | tf_op jit(solution)/shard_map/reduce_or | solution.py:36
  27.3 4.0 %collective-permute-start.3 = (bf16[512,768]{1,0:T(8,128)(2,1)S(1)}, bf16[512,768]{1,0:T(8,128)(2,1)S(1)}, u32[]{:S(2)}, u32[]{:S(2)}) collective-permute-start(bf16[512,768]{1,0:T(8,128)(2,1)S(1)} %collective-permute-done.1), channel_id=1, source_target_pairs={{0,1},{1,2},{2,3},{3,4},{4,5},{5,6},{6,7},{7,8},{8,9},{9,10},{10,1... | collective-permute-start | bytes 2359304 | tf_op jit(solution)/shard_map/ppermute | solution.py:11
  31.3 0.6 fusion.12
  31.9 0.6 fusion.11
  32.5 0.5 collective-permute-start.11
  33.0 10.4 %collective-permute-start.2 = (s32[512]{0:T(512)S(1)}, s32[512]{0:T(512)S(1)}, u32[]{:S(2)}, u32[]{:S(2)}) collective-permute-start(s32[512]{0:T(512)S(1)} %collective-permute-done), channel_id=1, source_target_pairs={{0,1},{1,2},{2,3},{3,4},{4,5},{5,6},{6,7},{7,8},{8,9},{9,10},{10,1... | collective-permute-start | bytes 6152 | tf_op jit(solution)/shard_map/ppermute | solution.py:11
  43.5 0.6 fusion.13
  44.3 0.5 collective-permute-done.6
  44.8 3.8 %fusion.4 = (bf16[512]{0:T(512)(128)(2,1)S(1)}, f32[512]{0:T(512)S(1)}, f32[512]{0:T(512)S(1)}, bf16[512]{0:T(512)(128)(2,1)S(1)}, f32[512]{0:T(512)S(1)}, /*ind...) fusion(s32[512]{0:T(512)S(1)} %collective-permute-done.2, pred[]{:T(512)} %get-tuple-element.19, ...), kind=kOutput, calls=%fused_computation.11 | convolution fusion | flops 407891968 | bytes 4741124 | tf_op jit(solution)/shard_map/dot_general | solution.py:21
  48.6 1.8 %collective-permute-start.9 = (bf16[512]{0:T(512)(128)(2,1)S(1)}, bf16[512]{0:T(512)(128)(2,1)S(1)}, u32[]{:S(2)}, u32[]{:S(2)}) collective-permute-start(bf16[512]{0:T(512)(128)(2,1)S(1)} %max.53), channel_id=1, source_target_pairs={{0,1},{1,2},{2,3},{3,4},{4,5},{5,6},{6,7},{7,8},{8,9},{9,10},{10,1... | collective-permute-start | bytes 3080 | tf_op jit(solution)/shard_map/ppermute | solution.py:11
  50.3 2.8 %collective-permute-start.12 = (bf16[512]{0:T(512)(128)(2,1)S(1)}, bf16[512]{0:T(512)(128)(2,1)S(1)}, u32[]{:S(2)}, u32[]{:S(2)}) collective-permute-start(bf16[512]{0:T(512)(128)(2,1)S(1)} %max.51), channel_id=1, source_target_pairs={{0,15},{1,0},{2,1},{3,2},{4,3},{5,4},{6,5},{7,6},{8,7},{9,8},{10,9... | collective-permute-start | bytes 3080 | tf_op jit(solution)/shard_map/ppermute | solution.py:11
  53.1 0.7 %fusion.10 = (bf16[512]{0:T(512)(128)(2,1)S(1)}, f32[512]{0:T(512)S(1)}) fusion(bf16[512,768]{1,0:T(8,128)(2,1)S(1)} %fusion.1, s32[512]{0:T(512)S(1)} %copy-done.2), kind=kOutput, calls=%fused_computation.28 | convolution fusion | flops 403700736 | bytes 791552 | tf_op jit(solution)/shard_map/dot_general | solution.py:21
  53.8 0.5 collective-permute-done.9
  54.3 1.9 %collective-permute-start.10 = (bf16[512]{0:T(512)(128)(2,1)S(1)}, bf16[512]{0:T(512)(128)(2,1)S(1)}, u32[]{:S(2)}, u32[]{:S(2)}) collective-permute-start(bf16[512]{0:T(512)(128)(2,1)S(1)} %max.52), channel_id=1, source_target_pairs={{0,14},{1,15},{2,0},{3,1},{4,2},{5,3},{6,4},{7,5},{8,6},{9,7},{10,... | collective-permute-start | bytes 3080 | tf_op jit(solution)/shard_map/ppermute | solution.py:11
  56.4 0.6 maximum_maximum_fusion
  57.0 0.9 %collective-permute-done.10 = bf16[512]{0:T(512)(128)(2,1)S(1)} collective-permute-done((bf16[512]{0:T(512)(128)(2,1)S(1)}, bf16[512]{0:T(512)(128)(2,1)S(1)}, u32[]{:S(2)}, u32[]{:S(2)}) %collective-permute-start.10) | collective-permute-done | bytes 1056 | tf_op jit(solution)/shard_map/ppermute | solution.py:11
  57.9 4.7 %collective-permute-done.13 = bf16[512]{0:T(512)(128)(2,1)S(1)} collective-permute-done((bf16[512]{0:T(512)(128)(2,1)S(1)}, bf16[512]{0:T(512)(128)(2,1)S(1)}, u32[]{:S(2)}, u32[]{:S(2)}) %collective-permute-start.13) | collective-permute-done | bytes 1056 | tf_op jit(solution)/shard_map/ppermute | solution.py:11
  62.6 0.6 maximum_maximum_fusion.1
  (26 shorter events, 0.6 us)
Async XLA Ops:
  0.6 1.5 %copy-start = (bf16[512,768]{1,0:T(8,128)(2,1)S(1)}, bf16[512,768]{1,0:T(8,128)(2,1)}, u32[]{:S(2)}) copy-start(bf16[512,768]{1,0:T(8,128)(2,1)} %param.3) | copy-start | bytes 2359300
  0.6 21.4 %copy-start.2 = (s32[512]{0:T(512)S(1)}, s32[512]{0:T(512)}, u32[]{:S(2)}) copy-start(s32[512]{0:T(512)} %param.4) | copy-start | bytes 6148
  0.6 25.8 %copy-start.1 = (s32[16,4]{0,1:T(4,128)S(1)}, s32[16,4]{0,1:T(4,128)}, u32[]{:S(2)}) copy-start(s32[16,4]{0,1:T(4,128)} %param.5) | copy-start | bytes 772
  2.3 15.0 %collective-permute-start.5 = (bf16[512,768]{1,0:T(8,128)(2,1)S(1)}, bf16[512,768]{1,0:T(8,128)(2,1)S(1)}, u32[]{:S(2)}, u32[]{:S(2)}) collective-permute-start(bf16[512,768]{1,0:T(8,128)(2,1)S(1)} %fusion.1), channel_id=1, source_target_pairs={{0,15},{1,0},{2,1},{3,2},{4,3},{5,4},{6,5},{7,6},{8,7},{9,8},{10,9... | collective-permute-start | bytes 2359304 | tf_op jit(solution)/shard_map/ppermute | solution.py:11
  7.8 19.5 %collective-permute-start.1 = (bf16[512,768]{1,0:T(8,128)(2,1)S(1)}, bf16[512,768]{1,0:T(8,128)(2,1)S(1)}, u32[]{:S(2)}, u32[]{:S(2)}) collective-permute-start(bf16[512,768]{1,0:T(8,128)(2,1)S(1)} %fusion.1), channel_id=1, source_target_pairs={{0,1},{1,2},{2,3},{3,4},{4,5},{5,6},{6,7},{7,8},{8,9},{9,10},{10,1... | collective-permute-start | bytes 2359304 | tf_op jit(solution)/shard_map/ppermute | solution.py:11
  17.3 26.2 %collective-permute-start.7 = (bf16[512,768]{1,0:T(8,128)(2,1)S(1)}, bf16[512,768]{1,0:T(8,128)(2,1)S(1)}, u32[]{:S(2)}, u32[]{:S(2)}) collective-permute-start(bf16[512,768]{1,0:T(8,128)(2,1)S(1)} %collective-permute-done.5), channel_id=1, source_target_pairs={{0,15},{1,0},{2,1},{3,2},{4,3},{5,4},{6,5},{7,6},{8,7},{9,8},{10,9... | collective-permute-start | bytes 2359304 | tf_op jit(solution)/shard_map/ppermute | solution.py:11
  22.0 10.5 %collective-permute-start = (s32[512]{0:T(512)S(1)}, s32[512]{0:T(512)S(1)}, u32[]{:S(2)}, u32[]{:S(2)}) collective-permute-start(s32[512]{0:T(512)S(1)} %copy-done.2), channel_id=1, source_target_pairs={{0,1},{1,2},{2,3},{3,4},{4,5},{5,6},{6,7},{7,8},{8,9},{9,10},{10,1... | collective-permute-start | bytes 6152 | tf_op jit(solution)/shard_map/ppermute | solution.py:11
  23.6 9.5 %collective-permute-start.4 = (s32[512]{0:T(512)S(1)}, s32[512]{0:T(512)S(1)}, u32[]{:S(2)}, u32[]{:S(2)}) collective-permute-start(s32[512]{0:T(512)S(1)} %copy-done.2), channel_id=1, source_target_pairs={{0,15},{1,0},{2,1},{3,2},{4,3},{5,4},{6,5},{7,6},{8,7},{9,8},{10,9... | collective-permute-start | bytes 6152 | tf_op jit(solution)/shard_map/ppermute | solution.py:11
  26.5 22.1 %collective-permute-start.8 = (bf16[512]{0:T(512)(128)(2,1)S(1)}, bf16[512]{0:T(512)(128)(2,1)S(1)}, u32[]{:S(2)}, u32[]{:S(2)}) collective-permute-start(bf16[512]{0:T(512)(128)(2,1)S(1)} %broadcast_in_dim.11), channel_id=1, source_target_pairs={{0,1},{1,2},{2,3},{3,4},{4,5},{5,6},{6,7},{7,8},{8,9},{9,10},{10,1... | collective-permute-start | bytes 3080 | tf_op jit(solution)/shard_map/ppermute | solution.py:11
  27.3 17.5 %collective-permute-start.3 = (bf16[512,768]{1,0:T(8,128)(2,1)S(1)}, bf16[512,768]{1,0:T(8,128)(2,1)S(1)}, u32[]{:S(2)}, u32[]{:S(2)}) collective-permute-start(bf16[512,768]{1,0:T(8,128)(2,1)S(1)} %collective-permute-done.1), channel_id=1, source_target_pairs={{0,1},{1,2},{2,3},{3,4},{4,5},{5,6},{6,7},{7,8},{8,9},{9,10},{10,1... | collective-permute-start | bytes 2359304 | tf_op jit(solution)/shard_map/ppermute | solution.py:11
  32.5 17.8 %collective-permute-start.11 = (bf16[512]{0:T(512)(128)(2,1)S(1)}, bf16[512]{0:T(512)(128)(2,1)S(1)}, u32[]{:S(2)}, u32[]{:S(2)}) collective-permute-start(bf16[512]{0:T(512)(128)(2,1)S(1)} %broadcast_in_dim.11), channel_id=1, source_target_pairs={{0,15},{1,0},{2,1},{3,2},{4,3},{5,4},{6,5},{7,6},{8,7},{9,8},{10,9... | collective-permute-start | bytes 3080 | tf_op jit(solution)/shard_map/ppermute | solution.py:11
  33.0 11.3 %collective-permute-start.2 = (s32[512]{0:T(512)S(1)}, s32[512]{0:T(512)S(1)}, u32[]{:S(2)}, u32[]{:S(2)}) collective-permute-start(s32[512]{0:T(512)S(1)} %collective-permute-done), channel_id=1, source_target_pairs={{0,1},{1,2},{2,3},{3,4},{4,5},{5,6},{6,7},{7,8},{8,9},{9,10},{10,1... | collective-permute-start | bytes 6152 | tf_op jit(solution)/shard_map/ppermute | solution.py:11
  43.5 1.3 %collective-permute-start.6 = (s32[512]{0:T(512)S(1)}, s32[512]{0:T(512)S(1)}, u32[]{:S(2)}, u32[]{:S(2)}) collective-permute-start(s32[512]{0:T(512)S(1)} %collective-permute-done.4), channel_id=1, source_target_pairs={{0,15},{1,0},{2,1},{3,2},{4,3},{5,4},{6,5},{7,6},{8,7},{9,8},{10,9... | collective-permute-start | bytes 6152 | tf_op jit(solution)/shard_map/ppermute | solution.py:11
  48.6 5.7 %collective-permute-start.9 = (bf16[512]{0:T(512)(128)(2,1)S(1)}, bf16[512]{0:T(512)(128)(2,1)S(1)}, u32[]{:S(2)}, u32[]{:S(2)}) collective-permute-start(bf16[512]{0:T(512)(128)(2,1)S(1)} %max.53), channel_id=1, source_target_pairs={{0,1},{1,2},{2,3},{3,4},{4,5},{5,6},{6,7},{7,8},{8,9},{9,10},{10,1... | collective-permute-start | bytes 3080 | tf_op jit(solution)/shard_map/ppermute | solution.py:11
  50.3 5.9 %collective-permute-start.12 = (bf16[512]{0:T(512)(128)(2,1)S(1)}, bf16[512]{0:T(512)(128)(2,1)S(1)}, u32[]{:S(2)}, u32[]{:S(2)}) collective-permute-start(bf16[512]{0:T(512)(128)(2,1)S(1)} %max.51), channel_id=1, source_target_pairs={{0,15},{1,0},{2,1},{3,2},{4,3},{5,4},{6,5},{7,6},{8,7},{9,8},{10,9... | collective-permute-start | bytes 3080 | tf_op jit(solution)/shard_map/ppermute | solution.py:11
  54.3 3.6 %collective-permute-start.10 = (bf16[512]{0:T(512)(128)(2,1)S(1)}, bf16[512]{0:T(512)(128)(2,1)S(1)}, u32[]{:S(2)}, u32[]{:S(2)}) collective-permute-start(bf16[512]{0:T(512)(128)(2,1)S(1)} %max.52), channel_id=1, source_target_pairs={{0,14},{1,15},{2,0},{3,1},{4,2},{5,3},{6,4},{7,5},{8,6},{9,7},{10,... | collective-permute-start | bytes 3080 | tf_op jit(solution)/shard_map/ppermute | solution.py:11
  56.3 6.3 %collective-permute-start.13 = (bf16[512]{0:T(512)(128)(2,1)S(1)}, bf16[512]{0:T(512)(128)(2,1)S(1)}, u32[]{:S(2)}, u32[]{:S(2)}) collective-permute-start(bf16[512]{0:T(512)(128)(2,1)S(1)} %max.50), channel_id=1, source_target_pairs={{0,2},{1,3},{2,4},{3,5},{4,6},{5,7},{6,8},{7,9},{8,10},{9,11},{10,... | collective-permute-start | bytes 3080 | tf_op jit(solution)/shard_map/ppermute | solution.py:11
where the time goes:
time: 63.3 us; the launch traced here: 63.2 us
  starting transfers between devices  36.2 us (57%)
  waiting for transfers between devices  16.3 us (26%)
  matrix products  6.25 us (10%)
  other arithmetic  3.63 us (6%)
  between operations  0.73 us (1%)
    ppermute x14, starting transfers between devices, from_behind(): return lax.ppermute(x, axis, [(i, (i + by) % peers) for i in range(peers)])  36.2 us
    ppermute x14, waiting for transfers between devices, from_behind(): return lax.ppermute(x, axis, [(i, (i + by) % peers) for i in range(peers)])  16.3 us
    dot_general x5, matrix products, pair_scores(): lax.dot_general(unit_rows, unit_cols, (((1,), (1,)), ((), ())), preferred...  6.25 us
    reduce_sum x1, other arithmetic, normalize(): jnp.sum(values * values, axis=-1, keepdims=True) + 1e-06  1.43 us
  transfers between devices with their start and end apart: 14, of which 6 were waited for; matrix products, arithmetic and copies ran while one was open for 12% of the time, Pallas kernels for 0%

commit v1 on v0

v1 whole, which is shorter than its diff:
```python
import functools

import jax
import jax.numpy as jnp
from jax import lax
from jax.experimental import pallas as pl
from jax.experimental.pallas import tpu as pltpu
from jax.sharding import PartitionSpec as P

MESH = pl.DeviceIdType.MESH
LANES = 128


def normalize(embeddings):
    values = embeddings.astype(jnp.float32)
    inverse = lax.rsqrt(jnp.sum(values * values, axis=-1, keepdims=True) + 1e-06)
    return (values * inverse).astype(jnp.bfloat16)


def kernel(blocks, chunk, emb_ref, order_ref, list_ref, out_ref, unit, unit_t, partner, partner_t,
           visit, order_v, order_p, spread, own_acc, par_acc, vis_acc, par_in, vis_in,
           send_sem, recv_sem, small_send, small_recv):
    rows = emb_ref.shape[0]
    chunks = rows // chunk
    group = lax.axis_index("groups")
    me = lax.axis_index("blk")
    odd = lax.rem(me, 2)
    mate = me + 1 - 2 * odd
    above = lax.rem(me + 2, blocks)
    below = lax.rem(me + blocks - 2, blocks)
    target = jnp.where(odd == 1, above, below)
    source = jnp.where(odd == 1, below, above)

    barrier = pltpu.get_barrier_semaphore()
    for peer in (mate, above, below):
        pl.semaphore_signal(barrier, inc=1, device_id=(group, peer), device_id_type=MESH)

    for c in range(chunks):
        part = pl.ds(c * chunk, chunk)
        unit[part, :] = normalize(emb_ref[part, :])

    pl.semaphore_wait(barrier, 3)

    def remote(src, dst, send, recv, peer):
        return pltpu.make_async_remote_copy(
            src_ref=src, dst_ref=dst, send_sem=send, recv_sem=recv,
            device_id=(group, peer), device_id_type=MESH,
        )

    order_copies = [
        remote(order_ref, order_v, small_send.at[0], small_recv.at[0], target),
        remote(order_ref, order_p, small_send.at[1], small_recv.at[1], mate),
    ]
    block_copies = []
    for c in range(chunks):
        part = pl.ds(c * chunk, chunk)
        block_copies.append(
            remote(unit.at[part], visit.at[part], send_sem.at[c], recv_sem.at[c], target)
        )
    mate_copy = remote(unit, partner, send_sem.at[chunks], recv_sem.at[chunks], mate)
    order_copies[0].start()
    block_copies[0].start()
    order_copies[1].start()
    mate_copy.start()
    for copy in block_copies[1:]:
        copy.start()

    low = jnp.float32(-1.0)

    def listed(block, entry):
        line = list_ref[pl.ds(block, 1), :]
        return jnp.max(jnp.where(line == entry, 1, 0), axis=1, keepdims=True) > 0

    def spread_order(ref):
        spread[...] = jnp.transpose(jnp.broadcast_to(ref[...], (LANES, rows)))

    def pair(left, left_part, right_t, right_order):
        scores = jnp.dot(left, right_t, preferred_element_type=jnp.float32)
        left_order = spread[left_part, :]
        ups, downs, wide_up, wide_down = [], [], None, None
        for g in range(rows // LANES):
            lanes = slice(g * LANES, (g + 1) * LANES)
            tile = scores[:, lanes]
            other = right_order[:, lanes]
            up = jnp.where(left_order < other, tile, low)
            down = jnp.where(left_order > other, tile, low)
            ups.append(jnp.max(up, axis=0, keepdims=True))
            downs.append(jnp.max(down, axis=0, keepdims=True))
            wide_up = up if g == 0 else jnp.maximum(wide_up, up)
            wide_down = down if g == 0 else jnp.maximum(wide_down, down)
        return jnp.concatenate(ups, 1), jnp.concatenate(downs, 1), wide_up, wide_down

    def fold(ref, line, values):
        ref[line:line + 1, :] = jnp.maximum(ref[line:line + 1, :], values)

    def narrow(values):
        return jnp.max(jnp.transpose(values), axis=0, keepdims=True)

    for ref in (own_acc, par_acc, vis_acc):
        ref[...] = jnp.full(ref.shape, low)

    my_order = order_ref[...]
    unit_t[...] = jnp.transpose(unit[...])
    spread_order(order_ref)
    for c in range(chunks):
        part = pl.ds(c * chunk, chunk)
        up, down, _, _ = pair(unit[part, :], part, unit_t[...], my_order)
        fold(own_acc, 0, up)
        fold(own_acc, 1, down)

    order_copies[1].wait_recv()
    mate_copy.wait_recv()
    own_has_mate = listed(me, mate)
    mate_has_own = listed(mate, me)

    @pl.when(odd == 1)
    def _():
        spread_order(order_p)
        for c in range(chunks):
            part = pl.ds(c * chunk, chunk)
            up, down, wide_up, wide_down = pair(partner[part, :], part, unit_t[...], my_order)
            fold(own_acc, 0, jnp.where(own_has_mate, up, low))
            fold(own_acc, 1, jnp.where(mate_has_own, down, low))
            lanes = slice(c * chunk, (c + 1) * chunk)
            par_acc[1:2, lanes] = jnp.where(own_has_mate, narrow(wide_up), low)
            par_acc[0:1, lanes] = jnp.where(mate_has_own, narrow(wide_down), low)

    @pl.when(odd == 0)
    def _():
        partner_t[...] = jnp.transpose(partner[...])

    order_copies[0].wait_recv()
    spread_order(order_v)
    own_has_vis = listed(me, source)
    vis_has_own = listed(source, me)
    mate_has_vis = listed(mate, source)
    vis_has_mate = listed(source, mate)
    for c in range(chunks):
        part = pl.ds(c * chunk, chunk)
        lanes = slice(c * chunk, (c + 1) * chunk)
        block_copies[c].wait_recv()
        up, down, wide_up, wide_down = pair(visit[part, :], part, unit_t[...], my_order)
        fold(own_acc, 0, jnp.where(own_has_vis, up, low))
        fold(own_acc, 1, jnp.where(vis_has_own, down, low))
        vis_acc[1:2, lanes] = jnp.where(own_has_vis, narrow(wide_up), low)
        vis_acc[0:1, lanes] = jnp.where(vis_has_own, narrow(wide_down), low)

        @pl.when(odd == 0)
        def _():
            up, down, wide_up, wide_down = pair(visit[part, :], part, partner_t[...], order_p[...])
            fold(par_acc, 0, jnp.where(mate_has_vis, up, low))
            fold(par_acc, 1, jnp.where(vis_has_mate, down, low))
            vis_acc[1:2, lanes] = jnp.maximum(
                vis_acc[1:2, lanes], jnp.where(mate_has_vis, narrow(wide_up), low)
            )
            vis_acc[0:1, lanes] = jnp.maximum(
                vis_acc[0:1, lanes], jnp.where(vis_has_mate, narrow(wide_down), low)
            )

    back = [
        remote(vis_acc, vis_in, small_send.at[2], small_recv.at[2], source),
        remote(par_acc, par_in, small_send.at[3], small_recv.at[3], mate),
    ]
    for copy in back:
        copy.start()
    for copy in order_copies + block_copies + [mate_copy]:
        copy.wait_send()
    back[1].wait_recv()
    best = jnp.maximum(own_acc[...], par_in[...])
    back[0].wait_recv()
    out_ref[...] = jnp.maximum(best, vis_in[...])
    for copy in back:
        copy.wait_send()


def local(blocks, embeddings, doc_order, neighbours):
    rows, width = embeddings.shape
    chunk = LANES
    chunks = rows // chunk
    vmem = pl.BlockSpec(memory_space=pltpu.VMEM)
    block = pltpu.VMEM((rows, width), jnp.bfloat16)
    block_t = pltpu.VMEM((width, rows), jnp.bfloat16)
    line = pltpu.VMEM((1, rows), jnp.int32)
    best = pltpu.VMEM((2, rows), jnp.float32)
    out = pl.pallas_call(
        functools.partial(kernel, blocks, chunk),
        out_shape=jax.ShapeDtypeStruct((2, rows), jnp.float32),
        in_specs=[vmem] * 3,
        out_specs=vmem,
        scratch_shapes=[
            block, block_t, block, block_t, block, line, line,
            pltpu.VMEM((rows, LANES), jnp.int32),
            best, best, best, best, best,
            pltpu.SemaphoreType.DMA((chunks + 1,)),
            pltpu.SemaphoreType.DMA((chunks + 1,)),
            pltpu.SemaphoreType.DMA((4,)),
            pltpu.SemaphoreType.DMA((4,)),
        ],
        compiler_params=pltpu.CompilerParams(
            collective_id=0, has_side_effects=True, vmem_limit_bytes=32 * 1024 * 1024
        ),
    )(embeddings, doc_order.reshape(1, rows), neighbours)
    return out[0], out[1].astype(jnp.bfloat16)


def solution(mesh):
    placed = (P(("groups", "blk"), None), P(("groups", "blk")), P("groups", None))
    return jax.shard_map(
        functools.partial(local, mesh.shape["blk"]),
        mesh=mesh,
        in_specs=placed,
        out_specs=(P(("groups", "blk")), P(("groups", "blk"))),
        check_vma=False,
    )
```

time: 63.3 us -> 29.1 us (0.46)
  starting transfers between devices: 36.2 us -> 0 us
  Pallas kernels: 0 us -> 25.2 us
  waiting for transfers between devices: 16.3 us -> 0 us
  matrix products: 6.25 us -> 0 us
  other arithmetic: 3.63 us -> 0 us
  local copies, waits for them, and re-layouts: 0.02 us -> 3.06 us
    ppermute x14 -> x0, starting transfers between devices: 36.2 us -> none  [from_behind(): return lax.ppermute(x, axis, [(i, (i + by) % peers) for i in range(peers)])]
    pallas_call x0 -> x1, Pallas kernels: none -> 25.2 us  [local(): pl.pallas_call(functools.partial(kernel, blocks, chunk), out_shape=jax.Sh...]
    ppermute x14 -> x0, waiting for transfers between devices: 16.3 us -> none  [from_behind(): return lax.ppermute(x, axis, [(i, (i + by) % peers) for i in range(peers)])]
    dot_general x5 -> x0, matrix products: 6.25 us -> none  [pair_scores(): lax.dot_general(unit_rows, unit_cols, (((1,), (1,)), ((), ())), preferred...]
    unnamed x6 -> x5, local copies, waits for them, and re-layouts: 0.01 us -> 1.9 us
    reduce_sum x1 -> x0, other arithmetic: 1.43 us -> none  [normalize(): jnp.sum(values * values, axis=-1, keepdims=True) + 1e-06]
    max x6 -> x0, other arithmetic: 1.18 us -> none  [the longest x1 0.58 us: visit(): jnp.maximum(row_best, jnp.max(masked, axis=1))]
    slice x0 -> x2, local copies, waits for them, and re-layouts: none -> 1.16 us  [local(): return (out[0], out[1].astype(jnp.bfloat16))]
  transfers between devices with their start and end apart: 14 -> 0, of which waited for: 6 -> 0; matrix products, arithmetic and copies ran while one was open for 12% -> 0% of each run, Pallas kernels for 0% -> 0%
where the time goes in v1:
time: 29.1 us; the launch traced here: 28.9 us
  Pallas kernels  25.2 us (87%)
  local copies, waits for them, and re-layouts  3.06 us (11%)
  between operations  0.65 us (2%)
    pallas_call x1, Pallas kernels, local(): pl.pallas_call(functools.partial(kernel, blocks, chunk), out_shape=jax.Sh...  25.2 us
    unnamed x5, local copies, waits for them, and re-layouts  1.9 us
    slice x2, local copies, waits for them, and re-layouts, local(): return (out[0], out[1].astype(jnp.bfloat16))  1.16 us

profile of v1, /device:TPU:0, one launch (start us, length us, event | category | flops | bytes accessed | tf_op | source)
XLA Modules:
  0.0 28.9 jit_solution(3407276871666019635)
XLA Ops:
  0.6 0.0 copy-start.1
  0.6 0.8 %copy.5.list_ref = s32[16,4]{1,0:T(8,128)S(1)} copy(s32[16,4]{0,1:T(4,128)} %param.5) | data formatting | bytes 512 | tf_op args[2]
  1.4 0.0 copy-done.1
  1.4 0.0 copy-start
  1.4 1.1 %copy-done = bf16[512,768]{1,0:T(8,128)(2,1)S(1)} copy-done((bf16[512,768]{1,0:T(8,128)(2,1)S(1)}, bf16[512,768]{1,0:T(8,128)(2,1)}, u32[]{:S(2)}) %copy-start) | copy-done | bytes 786456
  2.5 25.2 %shard_map.50 = f32[2,512]{1,0:T(2,128)S(1)} custom-call(bf16[512,768]{1,0:T(8,128)(2,1)S(1)} %copy-done, s32[1,512]{1,0:T(1,128)S(1)} %bitcast.2, s32[16,4]{1,0:T(8,128)S(1)} %copy.5.list_ref), custom_call_target="tpu_custom_call" | custom-call | tf_op jit(solution)/shard_map/pallas_call | solution.py:185
  27.8 0.6 %fusion = bf16[512]{0:T(512)(128)(2,1)} fusion(f32[2,512]{1,0:T(2,128)S(1)} %shard_map.50), kind=kLoop, calls=%fused_computation.1 | loop fusion | bytes 2048 | tf_op jit(solution)/shard_map/slice | solution.py:203
  28.3 0.6 %slice.7 = f32[1,512]{1,0:T(1,128)} slice(f32[2,512]{1,0:T(2,128)S(1)} %shard_map.50), slice={[0:1], [0:512]} | slice | bytes 4096 | tf_op jit(solution)/shard_map/slice | solution.py:203
Async XLA Ops:
  0.6 0.8 %copy-start.1 = (s32[512]{0:T(512)S(1)}, s32[512]{0:T(512)}, u32[]{:S(2)}) copy-start(s32[512]{0:T(512)} %param.4) | copy-start | bytes 6148
  1.4 1.1 %copy-start = (bf16[512,768]{1,0:T(8,128)(2,1)S(1)}, bf16[512,768]{1,0:T(8,128)(2,1)}, u32[]{:S(2)}) copy-start(bf16[512,768]{1,0:T(8,128)(2,1)} %emb_ref.1) | copy-start | bytes 2359300

commit v2 on v1

--- a/solution.py
+++ b/solution.py
@@ -17,8 +17,8 @@
     return (values * inverse).astype(jnp.bfloat16)
 
 
-def kernel(blocks, chunk, emb_ref, order_ref, list_ref, out_ref, unit, unit_t, partner, partner_t,
-           visit, order_v, order_p, spread, own_acc, par_acc, vis_acc, par_in, vis_in,
+def kernel(blocks, chunk, emb_hbm, order_hbm, list_hbm, out_ref, emb_ref, order_ref, list_ref,
+           fetch_sem, unit, unit_t, partner, partner_t, visit, order_v, order_p, spread, own_acc, par_acc, vis_acc, par_in, vis_in,
            send_sem, recv_sem, small_send, small_recv):
     rows = emb_ref.shape[0]
     chunks = rows // chunk
@@ -31,14 +31,26 @@
     target = jnp.where(odd == 1, above, below)
     source = jnp.where(odd == 1, below, above)
 
+    fetches = [
+        pltpu.make_async_copy(src, dst, fetch_sem.at[i])
+        for i, (src, dst) in enumerate(
+            ((emb_hbm, emb_ref), (order_hbm, order_ref), (list_hbm, list_ref))
+        )
+    ]
+    for fetch in fetches:
+        fetch.start()
+
     barrier = pltpu.get_barrier_semaphore()
     for peer in (mate, above, below):
         pl.semaphore_signal(barrier, inc=1, device_id=(group, peer), device_id_type=MESH)
 
+    fetches[0].wait()
     for c in range(chunks):
         part = pl.ds(c * chunk, chunk)
         unit[part, :] = normalize(emb_ref[part, :])
 
+    fetches[1].wait()
+    fetches[2].wait()
     pl.semaphore_wait(barrier, 3)
 
     def remote(src, dst, send, recv, peer):
@@ -68,8 +80,9 @@
     low = jnp.float32(-1.0)
 
     def listed(block, entry):
-        line = list_ref[pl.ds(block, 1), :]
-        return jnp.max(jnp.where(line == entry, 1, 0), axis=1, keepdims=True) > 0
+        lists = list_ref[...]
+        here = jnp.logical_and(lax.broadcasted_iota(jnp.int32, lists.shape, 1) == block, lists == entry)
+        return jnp.max(jnp.where(here, 1, 0), keepdims=True) > 0
 
     def spread_order(ref):
         spread[...] = jnp.transpose(jnp.broadcast_to(ref[...], (LANES, rows)))
@@ -173,6 +186,11 @@
         copy.wait_send()
 
 
+def finish(best_ref, earlier_ref, later_ref):
+    earlier_ref[...] = best_ref[0, :]
+    later_ref[...] = best_ref[1, :].astype(jnp.bfloat16)
+
+
 def local(blocks, embeddings, doc_order, neighbours):
     rows, width = embeddings.shape
     chunk = LANES
@@ -185,9 +203,11 @@
     out = pl.pallas_call(
         functools.partial(kernel, blocks, chunk),
         out_shape=jax.ShapeDtypeStruct((2, rows), jnp.float32),
-        in_specs=[vmem] * 3,
+        in_specs=[pl.BlockSpec(memory_space=pltpu.HBM)] * 3,
         out_specs=vmem,
         scratch_shapes=[
+            block, line, pltpu.VMEM(neighbours.shape[::-1], jnp.int32),
+            pltpu.SemaphoreType.DMA((3,)),
             block, block_t, block, block_t, block, line, line,
             pltpu.VMEM((rows, LANES), jnp.int32),
             best, best, best, best, best,
@@ -197,10 +217,19 @@
             pltpu.SemaphoreType.DMA((4,)),
         ],
         compiler_params=pltpu.CompilerParams(
-            collective_id=0, has_side_effects=True, vmem_limit_bytes=32 * 1024 * 1024
+            collective_id=0, has_side_effects=True, vmem_limit_bytes=60 * 1024 * 1024
         ),
-    )(embeddings, doc_order.reshape(1, rows), neighbours)
-    return out[0], out[1].astype(jnp.bfloat16)
+    )(embeddings, doc_order.reshape(1, rows), neighbours.T)
+    return pl.pallas_call(
+        finish,
+        out_shape=(
+            jax.ShapeDtypeStruct((rows,), jnp.float32),
+            jax.ShapeDtypeStruct((rows,), jnp.bfloat16),
+        ),
+        in_specs=[vmem],
+        out_specs=(vmem, vmem),
+        compiler_params=pltpu.CompilerParams(vmem_limit_bytes=60 * 1024 * 1024),
+    )(out)
 
 
 def solution(mesh):

time: 29.1 us -> 28 us (0.962)
  local copies, waits for them, and re-layouts: 3.06 us -> 0 us
  Pallas kernels: 25.2 us -> 27.1 us
    unnamed x5 -> x0, local copies, waits for them, and re-layouts: 1.9 us -> none
    pallas_call x0 -> x1, Pallas kernels: none -> 1.26 us  [local(): pl.pallas_call(finish, out_shape=(jax.ShapeDtypeStruct((rows,), jnp.float...]
    slice x2 -> x0, local copies, waits for them, and re-layouts: 1.16 us -> none  [local(): return (out[0], out[1].astype(jnp.bfloat16))]
    pallas_call x1, Pallas kernels: 25.2 us -> 25.9 us  [local(): pl.pallas_call(functools.partial(kernel, blocks, chunk), out_shape=jax.Sh...]
where the time goes in v2:
time: 28 us; the launch traced here: 27.8 us
  Pallas kernels  27.1 us (97%)
  between operations  0.64 us (2%)
    pallas_call x1, Pallas kernels, local(): pl.pallas_call(functools.partial(kernel, blocks, chunk), out_shape=jax.Sh...  25.9 us
    pallas_call x1, Pallas kernels, local(): pl.pallas_call(finish, out_shape=(jax.ShapeDtypeStruct((rows,), jnp.float...  1.26 us

profile of v2, /device:TPU:0, one launch (start us, length us, event | category | flops | bytes accessed | tf_op | source)
XLA Modules:
  0.0 27.8 jit_solution(15547139668009736630)
XLA Ops:
  0.6 25.9 %shard_map.50.best_ref = f32[2,512]{1,0:T(2,128)} custom-call(bf16[512,768]{1,0:T(8,128)(2,1)} %emb_hbm.1, s32[1,512]{1,0:T(1,128)} %bitcast.2, s32[4,16]{1,0:T(4,128)} %bitcast.3), custom_call_target="tpu_custom_call" | custom-call | tf_op jit(solution)/shard_map/pallas_call | solution.py:203
  26.5 1.3 %shard_map.51 = (f32[512]{0:T(512)}, bf16[512]{0:T(512)(128)(2,1)}) custom-call(f32[2,512]{1,0:T(2,128)} %shard_map.50.best_ref), custom_call_target="tpu_custom_call" | custom-call | tf_op jit(solution)/shard_map/pallas_call | solution.py:223

commit v3 on v2

--- a/solution.py
+++ b/solution.py
@@ -34,23 +34,25 @@
     fetches = [
         pltpu.make_async_copy(src, dst, fetch_sem.at[i])
         for i, (src, dst) in enumerate(
-            ((emb_hbm, emb_ref), (order_hbm, order_ref), (list_hbm, list_ref))
+            [(order_hbm, order_ref), (list_hbm, list_ref)]
+            + [(emb_hbm.at[pl.ds(c * chunk, chunk)], emb_ref.at[pl.ds(c * chunk, chunk)])
+               for c in range(chunks)]
         )
     ]
-    for fetch in fetches:
-        fetch.start()
+    for i in [2, 0, 1] + list(range(3, 2 + chunks)):
+        fetches[i].start()
 
     barrier = pltpu.get_barrier_semaphore()
     for peer in (mate, above, below):
         pl.semaphore_signal(barrier, inc=1, device_id=(group, peer), device_id_type=MESH)
 
+    def make_unit(c):
+        part = pl.ds(c * chunk, chunk)
+        fetches[2 + c].wait()
+        unit[part, :] = normalize(emb_ref[part, :])
+
+    make_unit(0)
     fetches[0].wait()
-    for c in range(chunks):
-        part = pl.ds(c * chunk, chunk)
-        unit[part, :] = normalize(emb_ref[part, :])
-
-    fetches[1].wait()
-    fetches[2].wait()
     pl.semaphore_wait(barrier, 3)
 
     def remote(src, dst, send, recv, peer):
@@ -72,10 +74,12 @@
     mate_copy = remote(unit, partner, send_sem.at[chunks], recv_sem.at[chunks], mate)
     order_copies[0].start()
     block_copies[0].start()
+    for c in range(1, chunks):
+        make_unit(c)
+        block_copies[c].start()
     order_copies[1].start()
     mate_copy.start()
-    for copy in block_copies[1:]:
-        copy.start()
+    fetches[1].wait()
 
     low = jnp.float32(-1.0)
 
@@ -207,7 +211,7 @@
         out_specs=vmem,
         scratch_shapes=[
             block, line, pltpu.VMEM(neighbours.shape[::-1], jnp.int32),
-            pltpu.SemaphoreType.DMA((3,)),
+            pltpu.SemaphoreType.DMA((chunks + 2,)),
             block, block_t, block, block_t, block, line, line,
             pltpu.VMEM((rows, LANES), jnp.int32),
             best, best, best, best, best,

time: 28 us -> 28 us (level)
  no operation moved by 1% of the time
where the time goes in v3:
time: 28 us; the launch traced here: 27.8 us
  Pallas kernels  27.2 us (97%)
  between operations  0.64 us (2%)
    pallas_call x1, Pallas kernels, local(): pl.pallas_call(functools.partial(kernel, blocks, chunk), out_shape=jax.Sh...  25.9 us
    pallas_call x1, Pallas kernels, local(): pl.pallas_call(finish, out_shape=(jax.ShapeDtypeStruct((rows,), jnp.float...  1.26 us

profile of v3, /device:TPU:0, one launch (start us, length us, event | category | flops | bytes accessed | tf_op | source)
XLA Modules:
  0.0 27.8 jit_solution(15554963627098984477)
XLA Ops:
  0.6 25.9 %shard_map.50.best_ref = f32[2,512]{1,0:T(2,128)} custom-call(bf16[512,768]{1,0:T(8,128)(2,1)} %emb_hbm.1, s32[1,512]{1,0:T(1,128)} %bitcast.2, s32[4,16]{1,0:T(4,128)} %bitcast.3), custom_call_target="tpu_custom_call" | custom-call | tf_op jit(solution)/shard_map/pallas_call | solution.py:207
  26.6 1.3 %shard_map.51 = (f32[512]{0:T(512)}, bf16[512]{0:T(512)(128)(2,1)}) custom-call(f32[2,512]{1,0:T(2,128)} %shard_map.50.best_ref), custom_call_target="tpu_custom_call" | custom-call | tf_op jit(solution)/shard_map/pallas_call | solution.py:227

commit v4 on v2

--- a/solution.py
+++ b/solution.py
@@ -202,7 +202,7 @@
     best = pltpu.VMEM((2, rows), jnp.float32)
     out = pl.pallas_call(
         functools.partial(kernel, blocks, chunk),
-        out_shape=jax.ShapeDtypeStruct((2, rows), jnp.float32),
+        out_shape=pltpu.VMEM((2, rows), jnp.float32),
         in_specs=[pl.BlockSpec(memory_space=pltpu.HBM)] * 3,
         out_specs=vmem,
         scratch_shapes=[
@@ -228,7 +228,7 @@
         ),
         in_specs=[vmem],
         out_specs=(vmem, vmem),
-        compiler_params=pltpu.CompilerParams(vmem_limit_bytes=60 * 1024 * 1024),
+        compiler_params=pltpu.CompilerParams(vmem_limit_bytes=1024 * 1024),
     )(out)
 
 

time: 28 us -> 26.7 us (0.954)
  Pallas kernels: 27.1 us -> 25.9 us
    pallas_call x1, Pallas kernels: 1.26 us -> 0.58 us  [local(): pl.pallas_call(finish, out_shape=(jax.ShapeDtypeStruct((rows,), jnp.float...]
    pallas_call x1, Pallas kernels: 25.9 us -> 25.3 us  [local(): pl.pallas_call(functools.partial(kernel, blocks, chunk), out_shape=pltpu....]
where the time goes in v4:
time: 26.7 us; the launch traced here: 26.5 us
  Pallas kernels  25.9 us (97%)
  between operations  0.64 us (2%)
    pallas_call x1, Pallas kernels, local(): pl.pallas_call(functools.partial(kernel, blocks, chunk), out_shape=pltpu....  25.3 us
    pallas_call x1, Pallas kernels, local(): pl.pallas_call(finish, out_shape=(jax.ShapeDtypeStruct((rows,), jnp.float...  0.58 us

profile of v4, /device:TPU:0, one launch (start us, length us, event | category | flops | bytes accessed | tf_op | source)
XLA Modules:
  0.0 26.5 jit_solution(14241941580507857832)
XLA Ops:
  0.6 25.3 %shard_map.50.best_ref = f32[2,512]{1,0:T(2,128)S(1)} custom-call(bf16[512,768]{1,0:T(8,128)(2,1)} %emb_hbm.1, s32[1,512]{1,0:T(1,128)} %bitcast.2, s32[4,16]{1,0:T(4,128)} %bitcast.3), custom_call_target="tpu_custom_call" | custom-call | tf_op jit(solution)/shard_map/pallas_call | solution.py:203
  25.9 0.6 %shard_map.51 = (f32[512]{0:T(512)}, bf16[512]{0:T(512)(128)(2,1)}) custom-call(f32[2,512]{1,0:T(2,128)S(1)} %shard_map.50.best_ref), custom_call_target="tpu_custom_call" | custom-call | tf_op jit(solution)/shard_map/pallas_call | solution.py:223

commit v5 on v4

--- a/solution.py
+++ b/solution.py
@@ -18,7 +18,7 @@
 
 
 def kernel(blocks, chunk, emb_hbm, order_hbm, list_hbm, out_ref, emb_ref, order_ref, list_ref,
-           fetch_sem, unit, unit_t, partner, partner_t, visit, order_v, order_p, spread, own_acc, par_acc, vis_acc, par_in, vis_in,
+           fetch_sem, unit, unit_t, partner, partner_t, visit, visit_unit, order_v, order_p, spread, own_acc, par_acc, vis_acc, par_in, vis_in,
            send_sem, recv_sem, small_send, small_recv):
     rows = emb_ref.shape[0]
     chunks = rows // chunk
@@ -44,13 +44,7 @@
     for peer in (mate, above, below):
         pl.semaphore_signal(barrier, inc=1, device_id=(group, peer), device_id_type=MESH)
 
-    fetches[0].wait()
-    for c in range(chunks):
-        part = pl.ds(c * chunk, chunk)
-        unit[part, :] = normalize(emb_ref[part, :])
-
     fetches[1].wait()
-    fetches[2].wait()
     pl.semaphore_wait(barrier, 3)
 
     def remote(src, dst, send, recv, peer):
@@ -67,15 +61,20 @@
     for c in range(chunks):
         part = pl.ds(c * chunk, chunk)
         block_copies.append(
-            remote(unit.at[part], visit.at[part], send_sem.at[c], recv_sem.at[c], target)
+            remote((unit if c else emb_hbm).at[part], visit.at[part], send_sem.at[c], recv_sem.at[c], target)
         )
     mate_copy = remote(unit, partner, send_sem.at[chunks], recv_sem.at[chunks], mate)
     order_copies[0].start()
     block_copies[0].start()
+    fetches[0].wait()
+    for c in range(chunks):
+        part = pl.ds(c * chunk, chunk)
+        unit[part, :] = normalize(emb_ref[part, :])
+        if c:
+            block_copies[c].start()
     order_copies[1].start()
     mate_copy.start()
-    for copy in block_copies[1:]:
-        copy.start()
+    fetches[2].wait()
 
     low = jnp.float32(-1.0)
 
@@ -152,7 +151,8 @@
         part = pl.ds(c * chunk, chunk)
         lanes = slice(c * chunk, (c + 1) * chunk)
         block_copies[c].wait_recv()
-        up, down, wide_up, wide_down = pair(visit[part, :], part, unit_t[...], my_order)
+        visit_unit[part, :] = visit[part, :] if c else normalize(visit[part, :])
+        up, down, wide_up, wide_down = pair(visit_unit[part, :], part, unit_t[...], my_order)
         fold(own_acc, 0, jnp.where(own_has_vis, up, low))
         fold(own_acc, 1, jnp.where(vis_has_own, down, low))
         vis_acc[1:2, lanes] = jnp.where(own_has_vis, narrow(wide_up), low)
@@ -160,7 +160,7 @@
 
         @pl.when(odd == 0)
         def _():
-            up, down, wide_up, wide_down = pair(visit[part, :], part, partner_t[...], order_p[...])
+            up, down, wide_up, wide_down = pair(visit_unit[part, :], part, partner_t[...], order_p[...])
             fold(par_acc, 0, jnp.where(mate_has_vis, up, low))
             fold(par_acc, 1, jnp.where(vis_has_mate, down, low))
             vis_acc[1:2, lanes] = jnp.maximum(
@@ -208,7 +208,7 @@
         scratch_shapes=[
             block, line, pltpu.VMEM(neighbours.shape[::-1], jnp.int32),
             pltpu.SemaphoreType.DMA((3,)),
-            block, block_t, block, block_t, block, line, line,
+            block, block_t, block, block_t, block, block, line, line,
             pltpu.VMEM((rows, LANES), jnp.int32),
             best, best, best, best, best,
             pltpu.SemaphoreType.DMA((chunks + 1,)),

time: 26.7 us -> 26.8 us (level)
  no operation moved by 1% of the time
where the time goes in v5:
time: 26.8 us; the launch traced here: 26.7 us
  Pallas kernels  26.1 us (97%)
  between operations  0.64 us (2%)
    pallas_call x1, Pallas kernels, local(): pl.pallas_call(functools.partial(kernel, blocks, chunk), out_shape=pltpu....  25.5 us
    pallas_call x1, Pallas kernels, local(): pl.pallas_call(finish, out_shape=(jax.ShapeDtypeStruct((rows,), jnp.float...  0.58 us

profile of v5, /device:TPU:0, one launch (start us, length us, event | category | flops | bytes accessed | tf_op | source)
XLA Modules:
  0.0 26.7 jit_solution(10804751503466402640)
XLA Ops:
  0.6 25.5 %shard_map.50.best_ref = f32[2,512]{1,0:T(2,128)S(1)} custom-call(bf16[512,768]{1,0:T(8,128)(2,1)} %emb_hbm.1, s32[1,512]{1,0:T(1,128)} %bitcast.2, s32[4,16]{1,0:T(4,128)} %bitcast.3), custom_call_target="tpu_custom_call" | custom-call | tf_op jit(solution)/shard_map/pallas_call | solution.py:203
  26.1 0.6 %shard_map.51 = (f32[512]{0:T(512)}, bf16[512]{0:T(512)(128)(2,1)}) custom-call(f32[2,512]{1,0:T(2,128)S(1)} %shard_map.50.best_ref), custom_call_target="tpu_custom_call" | custom-call | tf_op jit(solution)/shard_map/pallas_call | solution.py:223
